TPU v7x, 32 devices: a whole 2x2x4 slice. The times are simulated.
32 devices in a mesh: dp: 8 (over z, x), ctx: 4 (over y, core).
Axes of the slice: x: 2, y: 2, z: 4, core: 2. Of those that a mesh axis runs over, the one named last changes fastest.
Arguments:
- layer_input: bfloat16 [8, 512, 4096], P('dp', 'ctx'), may hold values from -6 to 6
- queries: bfloat16 [8, 512, 4096], P('dp', 'ctx'), may hold values from -4.5 to 4.5
- keys_saved: bfloat16 [8, 512, 1024], P('dp', 'ctx'), may hold values from -4.5 to 4.5
- values_saved: bfloat16 [8, 512, 1024], P('dp', 'ctx'), may hold values from -6 to 6
- out_grad: bfloat16 [8, 512, 4096], P('dp', 'ctx'), may hold values from -6 to 6
- master_weight: float32 [4096, 6144], P('dp', 'ctx'), may hold values from -2 to 2
- first_moment: float32 [4096, 6144], P('dp', 'ctx'), may hold values from -100 to 100
- second_moment: float32 [4096, 6144], P('dp', 'ctx'), may hold values from 10 to 3000
Outputs:
- first_new: float32 [4096, 6144], P('dp', 'ctx')
- second_new: float32 [4096, 6144], P('dp', 'ctx')
- lamb_update: float32 [4096, 6144], P('dp', 'ctx')
- new_weights: bfloat16 [4096, 6144], P(None, 'ctx')
All inputs are finite; a program needn't handle non-finite values.
Results may differ from a plain program's by a relative error of at most 0.0095.
Values may be sent and summed in bfloat16 or wider, within the bound.
A program may use at most 128 MiB of HBM per device.

v0:
```python
import functools

import jax
import jax.numpy as jnp
from jax import lax
from jax.experimental import pallas as pl
from jax.experimental.pallas import tpu as pltpu
from jax.sharding import PartitionSpec as P

HEAD_DIM = 128
STEP = 100


beta_first = 0.9
beta_second = 0.999
adam_epsilon = 1e-06
decay_rate = 0.01
learn_rate = 0.01
masked_score = -1e30

MESH_ID = pl.DeviceIdType.MESH
SLOW = 4


def nt(left, right):
    return lax.dot_general(
        left, right, (((1,), (1,)), ((), ())), preferred_element_type=jnp.float32
    )


def nn(left, right):
    return jnp.dot(left, right, preferred_element_type=jnp.float32)


def head_kernel(group, block, q_ref, k_ref, v_ref, g_ref, out_ref, dk_acc, dv_acc):
    head = pl.program_id(1)
    length = q_ref.shape[0]
    scale = HEAD_DIM ** (-0.5)

    @pl.when(head == 0)
    def _():
        dk_acc[...] = jnp.zeros_like(dk_acc)
        dv_acc[...] = jnp.zeros_like(dv_acc)

    for start in range(0, length, block):
        keys = start + block
        query = q_ref[start:keys, :]
        grad = g_ref[start:keys, :]
        key = k_ref[:keys, :]
        value = v_ref[:keys, :]
        scores = nt(key, query) * scale
        row = lax.broadcasted_iota(jnp.int32, (keys, block), 0)
        column = lax.broadcasted_iota(jnp.int32, (keys, block), 1) + start
        scores = jnp.where(row <= column, scores, masked_score)
        weights = jnp.exp(scores - jnp.max(scores, axis=0, keepdims=True))
        probs = weights / jnp.sum(weights, axis=0, keepdims=True)
        probs_b = probs.astype(jnp.bfloat16)
        prob_grad = nt(value, grad)
        row_delta = jnp.sum(probs_b.astype(jnp.float32) * prob_grad, axis=0, keepdims=True)
        dscore = (probs * (prob_grad - row_delta)).astype(jnp.bfloat16)
        dq = lax.dot_general(
            dscore, key, (((0,), (0,)), ((), ())), preferred_element_type=jnp.float32
        )
        column_start = pl.multiple_of(head * HEAD_DIM, HEAD_DIM)
        out_ref[start:keys, pl.ds(column_start, HEAD_DIM)] = (dq * scale).astype(jnp.bfloat16)
        dk_acc[:keys, :] += nn(dscore, query)
        dv_acc[:keys, :] += nn(probs_b, grad)

    @pl.when(head == group - 1)
    def _():
        width = group * HEAD_DIM
        out_ref[:, width : width + HEAD_DIM] = (dk_acc[...] * scale).astype(jnp.bfloat16)
        out_ref[:, width + HEAD_DIM :] = dv_acc[...].astype(jnp.bfloat16)


def head_grads(query, key, value, grad):
    length = query.shape[0]
    kv_local = key.shape[1] // HEAD_DIM
    group = query.shape[1] // key.shape[1]
    query_spec = pl.BlockSpec((length, HEAD_DIM), lambda g, h: (0, g * group + h))
    key_spec = pl.BlockSpec((length, HEAD_DIM), lambda g, h: (0, g))
    return pl.pallas_call(
        functools.partial(head_kernel, group, min(256, length)),
        grid=(kv_local, group),
        in_specs=[query_spec, key_spec, key_spec, query_spec],
        out_specs=pl.BlockSpec((length, (group + 2) * HEAD_DIM), lambda g, h: (0, g)),
        out_shape=jax.ShapeDtypeStruct(
            (length, kv_local * (group + 2) * HEAD_DIM), jnp.bfloat16
        ),
        scratch_shapes=[pltpu.VMEM((length, HEAD_DIM), jnp.float32)] * 2,
        compiler_params=pltpu.CompilerParams(vmem_limit_bytes=40 * 1024 * 1024),
        cost_estimate=pl.CostEstimate(
            flops=10 * length * length * query.shape[1],
            bytes_accessed=8 * length * query.shape[1],
            transcendentals=length * length * kv_local * group,
        ),
        name="head_grads",
    )(query, key, value, grad)


def gather_kernel(slow, fast, chunks, tail, x_ref, out_ref, *sems):
    local_sem, p1s, p1r, x1s, x1r, x2s, x2r, p2s, p2r = sems
    me = lax.axis_index("dp")
    a = me // fast
    b = lax.rem(me, fast)
    lines = {"a": (a, slow, fast), "b": (b, fast, 1)}
    n_chunks = len(chunks)

    def neighbour(line, way):
        return me + way * lines[line][2]

    def can(line, way):
        pos, size, _ = lines[line]
        return pos + 1 < size if way > 0 else pos > 0

    barrier = pltpu.get_barrier_semaphore()
    for line in ("a", "b"):
        for way in (1, -1):

            @pl.when(can(line, way))
            def _(line=line, way=way):
                pl.semaphore_signal(
                    barrier,
                    inc=1,
                    device_id={"dp": neighbour(line, way)},
                    device_id_type=MESH_ID,
                )

    neighbours = sum(
        can(line, way).astype(jnp.int32) for line in ("a", "b") for way in (1, -1)
    )
    pl.semaphore_wait(barrier, neighbours)

    local = pltpu.make_async_copy(x_ref, out_ref.at[me], local_sem)
    local.start()

    def piece(origin, rows, own):
        start, size = rows
        if own:
            return x_ref.at[pl.ds(start, size)]
        return out_ref.at[origin, pl.ds(start, size)]

    def copy(line, way, origin, rows, own, send, recv):
        start, size = rows
        return pltpu.make_async_remote_copy(
            src_ref=piece(origin, rows, own),
            dst_ref=out_ref.at[origin, pl.ds(start, size)],
            send_sem=send,
            recv_sem=recv,
            device_id={"dp": neighbour(line, way)},
            device_id_type=MESH_ID,
        )

    pending = []

    def send(condition, *args):
        @pl.when(condition)
        def _():
            copy(*args).start()

        pending.append((condition, args))

    def both(first, second):
        return jnp.logical_and(first, second)

    def send_a1(step, c, way):
        origin_a = a - way * step
        inside = origin_a >= 0 if way > 0 else origin_a < slow
        d = 0 if way > 0 else 1
        i = (d * (slow - 1) + step) * n_chunks + c
        send(
            both(can("a", way), inside),
            "a", way, origin_a * fast + b, chunks[c], step == 0, p1s.at[i], p1r.at[i],
        )

    def recv_a1(step, c, way):
        origin_a = a - way * (step + 1)
        inside = origin_a >= 0 if way > 0 else origin_a < slow
        d = 0 if way > 0 else 1
        i = (d * (slow - 1) + step) * n_chunks + c

        @pl.when(inside)
        def _():
            copy("a", -way, origin_a * fast + b, chunks[c], False, p1s.at[i], p1r.at[i]).wait_recv()

        return inside, origin_a

    def send_b1(step, slot, c, way, present):
        origin_a = a + slot
        origin_b = b - way * step
        inside = origin_b >= 0 if way > 0 else origin_b < fast
        d = 0 if way > 0 else 1
        i = ((d * (fast - 1) + step) * (2 * slow - 1) + slot + slow - 1) * n_chunks + c
        send(
            both(present, both(can("b", way), inside)),
            "b", way, origin_a * fast + origin_b, chunks[c], step == 0 and slot == 0,
            x1s.at[i], x1r.at[i],
        )

    def recv_b1(step, slot, c, way):
        origin_a = a + slot
        present = both(origin_a >= 0, origin_a < slow)
        origin_b = b - way * (step + 1)
        inside = origin_b >= 0 if way > 0 else origin_b < fast
        d = 0 if way > 0 else 1
        i = ((d * (fast - 1) + step) * (2 * slow - 1) + slot + slow - 1) * n_chunks + c

        @pl.when(both(present, inside))
        def _():
            copy(
                "b", -way, origin_a * fast + origin_b, chunks[c], False, x1s.at[i], x1r.at[i]
            ).wait_recv()

        return present

    def send_b2(step, way):
        origin_b = b - way * step
        inside = origin_b >= 0 if way > 0 else origin_b < fast
        i = (0 if way > 0 else 1) * (fast - 1) + step
        send(
            both(can("b", way), inside),
            "b", way, a * fast + origin_b, tail, step == 0, x2s.at[i], x2r.at[i],
        )

    def recv_b2(step, way):
        origin_b = b - way * (step + 1)
        inside = origin_b >= 0 if way > 0 else origin_b < fast
        i = (0 if way > 0 else 1) * (fast - 1) + step

        @pl.when(inside)
        def _():
            copy("b", -way, a * fast + origin_b, tail, False, x2s.at[i], x2r.at[i]).wait_recv()

        return inside

    def send_a2(step, turn, way):
        origin_a = a - way * step
        inside = origin_a >= 0 if way > 0 else origin_a < slow
        origin_b = lax.rem(b + turn, fast)
        i = ((0 if way > 0 else 1) * (slow - 1) + step) * fast + turn
        send(
            both(can("a", way), inside),
            "a", way, origin_a * fast + origin_b, tail, step == 0 and turn == 0,
            p2s.at[i], p2r.at[i],
        )

    def recv_a2(step, turn, way):
        origin_a = a - way * (step + 1)
        inside = origin_a >= 0 if way > 0 else origin_a < slow
        origin_b = lax.rem(b + turn, fast)
        i = ((0 if way > 0 else 1) * (slow - 1) + step) * fast + turn

        @pl.when(inside)
        def _():
            copy(
                "a", -way, origin_a * fast + origin_b, tail, False, p2s.at[i], p2r.at[i]
            ).wait_recv()

    ways = (1, -1)
    always = a >= 0
    for c in range(n_chunks):
        for way in ways:
            send_a1(0, c, way)
        for way in ways:
            send_b1(0, 0, c, way, always)
    for way in ways:
        send_b2(0, way)
    for way in ways:
        send_a2(0, 0, way)
    for step in range(slow - 1):
        for c in range(n_chunks):
            for way in ways:
                present, _ = recv_a1(step, c, way)
                if step + 1 < slow - 1:
                    send_a1(step + 1, c, way)
                for way_b in ways:
                    send_b1(0, -way * (step + 1), c, way_b, present)
        if step == 0:
            for hop in range(fast - 1):
                for way in ways:
                    recv_b2(hop, way)
                    if hop + 1 < fast - 1:
                        send_b2(hop + 1, way)
            for turn in range(1, fast):
                for way in ways:
                    send_a2(0, turn, way)
        for turn in range(fast):
            for way in ways:
                recv_a2(step, turn, way)
                if step + 1 < slow - 1:
                    send_a2(step + 1, turn, way)
    slots = [0] + [sign * far for far in range(1, slow) for sign in (-1, 1)]
    for hop in range(fast - 1):
        for slot in slots:
            for c in range(n_chunks):
                for way in ways:
                    present = recv_b1(hop, slot, c, way)
                    if hop + 1 < fast - 1:
                        send_b1(hop + 1, slot, c, way, present)
    local.wait()
    for condition, args in pending:

        @pl.when(condition)
        def _(args=args):
            copy(*args).wait_send()


def gather_dp(shard, devices, collective_id, name):
    rows, columns = shard.shape
    slow = SLOW
    fast = devices // SLOW
    first = rows * 13 // 16 // 32 * 32
    chunks = ((0, first // 2), (first // 2, first // 2))
    tail = (first, rows - first)
    n_chunks = len(chunks)
    dma = pltpu.SemaphoreType.DMA
    sizes = (
        2 * (slow - 1) * n_chunks,
        2 * (fast - 1) * (2 * slow - 1) * n_chunks,
        2 * (fast - 1),
        2 * (slow - 1) * fast,
    )
    return pl.pallas_call(
        functools.partial(gather_kernel, slow, fast, chunks, tail),
        in_specs=[pl.BlockSpec(memory_space=pl.ANY)],
        out_specs=pl.BlockSpec(memory_space=pl.ANY),
        out_shape=jax.ShapeDtypeStruct((devices, rows, columns), shard.dtype),
        scratch_shapes=[dma] + [dma((size,)) for size in sizes for _ in range(2)],
        compiler_params=pltpu.CompilerParams(
            collective_id=collective_id, has_side_effects=True
        ),
        cost_estimate=pl.CostEstimate(
            flops=0, bytes_accessed=4 * devices * rows * columns, transcendentals=0
        ),
        name=name,
    )(shard)


def exchange_kernel(n_ctx, n_dp, widths, input_width, *refs):
    count = len(widths)
    sources, source_input = refs[:count], refs[count]
    targets, target_input = refs[count + 1 : 2 * count + 1], refs[2 * count + 1]
    ctx_send, ctx_recv, dp_send, dp_recv, local_sems = refs[2 * count + 2 :]
    dp = lax.axis_index("dp")
    ctx = lax.axis_index("ctx")
    rows = source_input.shape[0]
    barrier = pltpu.get_barrier_semaphore()
    for turn in range(1, n_ctx):
        pl.semaphore_signal(
            barrier, inc=1, device_id={"ctx": lax.rem(ctx + turn, n_ctx)}, device_id_type=MESH_ID
        )
    for turn in range(1, n_dp):
        pl.semaphore_signal(
            barrier, inc=1, device_id={"dp": lax.rem(dp + turn, n_dp)}, device_id_type=MESH_ID
        )
    pl.semaphore_wait(barrier, n_ctx + n_dp - 2)

    def source(i, peer):
        return sources[i].at[:, pl.ds(pl.multiple_of(peer * widths[i], 128), widths[i])]

    def source_columns(peer):
        return source_input.at[:, pl.ds(pl.multiple_of(peer * input_width, 128), input_width)]

    def row_block(i, owner):
        return targets[i].at[pl.ds(pl.multiple_of(owner * rows, 16), rows)]

    copies = []
    for turn in range(1, n_ctx):
        peer = lax.rem(ctx + turn, n_ctx)
        for i in range(count):
            k = i * (n_ctx - 1) + turn - 1
            copies.append(
                pltpu.make_async_remote_copy(
                    src_ref=source(i, peer),
                    dst_ref=row_block(i, ctx),
                    send_sem=ctx_send.at[k],
                    recv_sem=ctx_recv.at[k],
                    device_id={"ctx": peer},
                    device_id_type=MESH_ID,
                )
            )
            copies[-1].start()
    for turn in range(1, n_dp):
        peer = lax.rem(dp + turn, n_dp)
        copies.append(
            pltpu.make_async_remote_copy(
                src_ref=source_columns(peer),
                dst_ref=target_input.at[dp],
                send_sem=dp_send.at[turn - 1],
                recv_sem=dp_recv.at[turn - 1],
                device_id={"dp": peer},
                device_id_type=MESH_ID,
            )
        )
        copies[-1].start()
    owns = [
        pltpu.make_async_copy(source(i, ctx), row_block(i, ctx), local_sems.at[i])
        for i in range(count)
    ]
    owns.append(
        pltpu.make_async_copy(source_columns(dp), target_input.at[dp], local_sems.at[count])
    )
    for own in owns:
        own.start()
    for own in owns:
        own.wait()
    for turn in range(1, n_ctx):
        origin = lax.rem(ctx + n_ctx - turn, n_ctx)
        for i in range(count):
            k = i * (n_ctx - 1) + turn - 1
            pltpu.make_async_remote_copy(
                src_ref=source(i, origin),
                dst_ref=row_block(i, origin),
                send_sem=ctx_send.at[k],
                recv_sem=ctx_recv.at[k],
                device_id={"ctx": origin},
                device_id_type=MESH_ID,
            ).wait_recv()
    for turn in range(1, n_dp):
        origin = lax.rem(dp + n_dp - turn, n_dp)
        pltpu.make_async_remote_copy(
            src_ref=source_columns(origin),
            dst_ref=target_input.at[origin],
            send_sem=dp_send.at[turn - 1],
            recv_sem=dp_recv.at[turn - 1],
            device_id={"dp": origin},
            device_id_type=MESH_ID,
        ).wait_recv()
    for copy in copies:
        copy.wait_send()


def exchange(arrays, layer_input, n_ctx, n_dp):
    rows = layer_input.shape[0]
    widths = tuple(array.shape[1] // n_ctx for array in arrays)
    input_width = layer_input.shape[1] // n_dp
    dma = pltpu.SemaphoreType.DMA
    ctx_copies = len(arrays) * (n_ctx - 1)
    anywhere = pl.BlockSpec(memory_space=pl.ANY)
    return pl.pallas_call(
        functools.partial(exchange_kernel, n_ctx, n_dp, widths, input_width),
        in_specs=[anywhere] * (len(arrays) + 1),
        out_specs=[anywhere] * (len(arrays) + 1),
        out_shape=[
            jax.ShapeDtypeStruct((rows * n_ctx, width), jnp.bfloat16) for width in widths
        ]
        + [jax.ShapeDtypeStruct((n_dp, rows, input_width), jnp.bfloat16)],
        scratch_shapes=[
            dma((ctx_copies,)),
            dma((ctx_copies,)),
            dma((n_dp - 1,)),
            dma((n_dp - 1,)),
            dma((len(arrays) + 1,)),
        ],
        compiler_params=pltpu.CompilerParams(collective_id=3, has_side_effects=True),
        cost_estimate=pl.CostEstimate(
            flops=0, bytes_accessed=8 * rows * layer_input.shape[1], transcendentals=0
        ),
        name="exchange",
    )(*arrays, layer_input)


def total_kernel(n_ctx, n_dp, x_ref, out_ref, held_dp, part, held_ctx, *sems):
    dp_send, dp_recv, ctx_send, ctx_recv = sems
    dp = lax.axis_index("dp")
    ctx = lax.axis_index("ctx")
    stages = (
        ("dp", dp, n_dp, x_ref, held_dp, dp_send, dp_recv),
        ("ctx", ctx, n_ctx, part, held_ctx, ctx_send, ctx_recv),
    )
    barrier = pltpu.get_barrier_semaphore()
    for axis, me, size, *_ in stages:
        for turn in range(1, size):
            pl.semaphore_signal(
                barrier, inc=1, device_id={axis: lax.rem(me + turn, size)}, device_id_type=MESH_ID
            )
    pl.semaphore_wait(barrier, n_ctx + n_dp - 2)
    for axis, me, size, block, held, send, recv in stages:
        copies = [
            pltpu.make_async_remote_copy(
                src_ref=block,
                dst_ref=held.at[turn - 1],
                send_sem=send.at[turn - 1],
                recv_sem=recv.at[turn - 1],
                device_id={axis: lax.rem(me + turn, size)},
                device_id_type=MESH_ID,
            )
            for turn in range(1, size)
        ]
        for copy in copies:
            copy.start()
        for copy in copies:
            copy.wait()
        total = block[...]
        for turn in range(1, size):
            total += held[turn - 1]
        if axis == "dp":
            part[...] = total
        else:
            out_ref[...] = total


def total_over_devices(first, second, n_ctx, n_dp):
    rows = jnp.arange(8)[:, None]
    block = jnp.where(rows == 0, first, jnp.where(rows == 1, second, 0.0))
    block = jnp.broadcast_to(block, (8, 128)).astype(jnp.float32)
    dma = pltpu.SemaphoreType.DMA
    total = pl.pallas_call(
        functools.partial(total_kernel, n_ctx, n_dp),
        in_specs=[pl.BlockSpec(memory_space=pltpu.VMEM)],
        out_specs=pl.BlockSpec(memory_space=pltpu.VMEM),
        out_shape=jax.ShapeDtypeStruct((8, 128), jnp.float32),
        scratch_shapes=[
            pltpu.VMEM((n_dp - 1, 8, 128), jnp.float32),
            pltpu.VMEM((8, 128), jnp.float32),
            pltpu.VMEM((n_ctx - 1, 8, 128), jnp.float32),
            dma((n_dp - 1,)),
            dma((n_dp - 1,)),
            dma((n_ctx - 1,)),
            dma((n_ctx - 1,)),
        ],
        compiler_params=pltpu.CompilerParams(collective_id=4, has_side_effects=True),
        cost_estimate=pl.CostEstimate(flops=0, bytes_accessed=65536, transcendentals=0),
        name="total",
    )(block)
    return total[0, 0], total[1, 0]


def body(
    devices,
    heads_split,
    layer_input,
    queries,
    keys_saved,
    values_saved,
    out_grad,
    master_weight,
    first_moment,
    second_moment,
):
    weight_sq = jnp.sum(master_weight * master_weight)
    *heads, input_rows = exchange(
        (queries[0], keys_saved[0], values_saved[0], out_grad[0]),
        layer_input[0],
        heads_split,
        devices,
    )
    input_rows = lax.all_gather(input_rows, "ctx", axis=1, tiled=True)
    grouped = head_grads(*heads)
    grouped_all = gather_dp(grouped, devices, 1, "gather_grouped")
    gradient = lax.dot_general(
        input_rows,
        grouped_all,
        (((0, 1), (0, 1)), ((), ())),
        preferred_element_type=jnp.float32,
    )
    first_new = beta_first * first_moment + (1.0 - beta_first) * gradient
    second_new = beta_second * second_moment + (1.0 - beta_second) * gradient * gradient
    corr_first = 1.0 - beta_first**STEP
    corr_second = 1.0 - beta_second**STEP
    direction = (
        first_new / corr_first / (jnp.sqrt(second_new / corr_second) + adam_epsilon)
        + decay_rate * master_weight
    )
    update_sq = jnp.sum(direction * direction)
    weight_total, update_total = total_over_devices(
        weight_sq, update_sq, heads_split, devices
    )
    trust_ratio = jnp.sqrt(weight_total) / jnp.sqrt(update_total)
    lamb_update = trust_ratio * direction
    new_local = (master_weight - learn_rate * lamb_update).astype(jnp.bfloat16)
    new_weights = gather_dp(new_local, devices, 2, "gather_weights")
    return (first_new, second_new, lamb_update, new_weights.reshape(-1, new_local.shape[1]))


def solution(mesh):
    in_specs = (
        P("dp", "ctx", None),
        P("dp", "ctx", None),
        P("dp", "ctx", None),
        P("dp", "ctx", None),
        P("dp", "ctx", None),
        P("dp", "ctx"),
        P("dp", "ctx"),
        P("dp", "ctx"),
    )
    out_specs = (P("dp", "ctx"), P("dp", "ctx"), P("dp", "ctx"), P(None, "ctx"))
    return jax.shard_map(
        functools.partial(body, mesh.shape["dp"], mesh.shape["ctx"]),
        mesh=mesh,
        in_specs=in_specs,
        out_specs=out_specs,
        check_vma=False,
    )
```

profile of v0, /device:TPU:0, one launch (start us, length us, event | category | flops | bytes accessed | tf_op | source)
XLA Modules:
  0.0 370.8 jit_solution(68969487394511895)
XLA Ops:
  7.2 0.0 all-gather.2.cloned.1.call-start
  7.2 34.8 %exchange.1 = (bf16[512,1024]{1,0:T(8,128)(2,1)}, bf16[512,256]{1,0:T(8,128)(2,1)}, bf16[512,256]{1,0:T(8,128)(2,1)}, bf16[512,1024]{1,0:T(8,128)(2,1)}, bf16[8,128,512]{2,1,0:T(8,128)(2,1)}) custom-call(bf16[128,4096]{1,0:T(8,128)(2,1)} %bitcast.12, bf16[128,1024]{1,0:T(8,128)(2,1)} %bitcast.15, bf16[128,1024]{1,0:T(8,128)(2,1)} %bitcast.16, ...), custom_call_target="tpu_custom_call" | custom-call | bytes 4194304 | tf_op jit(solution)/shard_map/exchange/pallas_call | solution.py:440
  42.0 0.0 all-gather.2.cloned.1.call-update
  42.0 0.0 copy-start.1
  42.0 1.2 copy-done.1
  43.3 0.0 copy-start.2
  43.3 1.2 copy-done.2
  44.5 0.0 copy-start.3
  44.5 0.9 copy-done.3
  45.4 0.9 copy-done.4
  46.4 11.1 %head_grads.1.x_ref = bf16[512,1536]{1,0:T(8,128)(2,1)S(1)} custom-call(bf16[512,1024]{1,0:T(8,128)(2,1)S(1)} %copy-done.1, bf16[512,256]{1,0:T(8,128)(2,1)S(1)} %copy-done.3, bf16[512,256]{1,0:T(8,128)(2,1)S(1)} %copy-done.4, bf16[512,1024]{1,0:T(8,128)(2,1)S(1)} %copy-done.2), custom_call_target="tpu_custom_call" | custom-call | flops 2684354560 | bytes 4194304 | tf_op jit(solution)/shard_map/head_grads/pallas_call | solution.py:82
  57.5 0.0 copy-start
  57.5 1.1 copy-done
  58.6 127.7 %gather_grouped.1 = bf16[8,512,1536]{2,1,0:T(8,128)(2,1)} custom-call(bf16[512,1536]{1,0:T(8,128)(2,1)} %copy-done), custom_call_target="tpu_custom_call" | custom-call | bytes 25165824 | tf_op jit(solution)/shard_map/gather_grouped/pallas_call | solution.py:323
  186.4 0.0 all-gather.2.cloned.1.call-done
  186.4 0.0 copy-done.5
  186.4 17.5 %multiply_reduce_fusion = (f32[]{:T(128)}, f32[512,1536]{1,0:T(8,128)}, f32[512,1536]{1,0:T(8,128)}, f32[512,1536]{1,0:T(8,128)}, f32[]{:T(128)}) fusion(f32[512,1536]{1,0:T(8,128)S(1)} %copy-done.5, f32[512,1536]{1,0:T(8,128)} %param.15, f32[512,1536]{1,0:T(8,128)} %param.14, bf16[8,512,512]{2,1,0:T(8,128)(2,1)} %all-gather.2.cloned.1.call-done, ...), kind=kOutput, calls=%fused_computation.4 | convolution fusion | flops 6455820288 | bytes 35651592 | tf_op jit(solution)/shard_map/dot_general | solution.py:551
  203.9 1.3 compare_select_fusion.1
  205.3 0.7 broadcast_in_dim.21.x_ref
  205.9 11.8 %total.1 = f32[8,128]{1,0:T(8,128)} custom-call(f32[8,128]{1,0:T(8,128)} %broadcast_in_dim.21.x_ref), custom_call_target="tpu_custom_call" | custom-call | bytes 65536 | tf_op jit(solution)/shard_map/total/pallas_call | solution.py:508
  217.8 1.3 fusion.2
  220.5 4.8 %subtract_convert_fusion = (bf16[512,1536]{1,0:T(8,128)(2,1)}, f32[512,1536]{1,0:T(8,128)}) fusion(f32[512,1536]{1,0:T(8,128)S(1)} %copy-done.5, f32[512,1536]{1,0:T(8,128)} %get-tuple-element.17, f32[]{:T(128)} %bitcast.6), kind=kLoop, calls=%fused_computation.3 | loop fusion | flops 3145728 | bytes 11010052 | tf_op jit(solution)/shard_map/convert_element_type | solution.py:571
  225.3 128.2 %gather_weights.1 = bf16[8,512,1536]{2,1,0:T(8,128)(2,1)} custom-call(bf16[512,1536]{1,0:T(8,128)(2,1)} %get-tuple-element.14.x_ref), custom_call_target="tpu_custom_call" | custom-call | bytes 25165824 | tf_op jit(solution)/shard_map/gather_weights/pallas_call | solution.py:323
  353.5 10.5 %copy.15 = bf16[4096,1536]{1,0:T(8,128)(2,1)} copy(bf16[4096,1536]{1,0:T(8,128)(2,1)} %bitcast.11) | data formatting | bytes 25165824
  (2 shorter events, 0.0 us)
Async XLA Ops:
  7.2 179.3 %all-gather.2.cloned.1.call-start = ((), (), s32[]{:S(2)}) async-start(), calls=%async_computation | async-start | bytes 5242880 | tf_op jit(solution)/shard_map/all_gather | solution.py:548
  42.0 1.2 copy-start.1
  43.3 1.2 copy-start.2
  44.5 0.9 copy-start.3
  45.4 0.9 copy-start.4
  57.5 1.1 copy-start
  58.6 127.8 %copy-start.5 = (f32[512,1536]{1,0:T(8,128)S(1)}, f32[512,1536]{1,0:T(8,128)}, u32[]{:S(2)}) copy-start(f32[512,1536]{1,0:T(8,128)} %param.13) | copy-start | bytes 9437188
Sparse Core Ops, SparseCore 0:
  42.2 33.7 all-gather.1
where the time goes:
time: 371 us
  Pallas kernels  314 us (85%)
  local copies, waits for them, and re-layouts  17.9 us (5%)
  matrix products  17.5 us (5%)
  between operations  15.5 us (4%)
  other arithmetic  6.16 us (2%)
    pallas_call x2, Pallas kernels, gather_dp(): pl.pallas_call(functools.partial(gather_kernel, slow, fast, chunks, tail)...  256 us
    pallas_call x1, Pallas kernels, exchange(): pl.pallas_call(functools.partial(exchange_kernel, n_ctx, n_dp, widths, in...  34.8 us
    dot_general x1, matrix products, body(): lax.dot_general(input_rows, grouped_all, (((0, 1), (0, 1)), ((), ())), pr...  17.5 us
    unnamed x13, local copies, waits for them, and re-layouts  15.9 us
    pallas_call x1, Pallas kernels, total_over_devices(): pl.pallas_call(functools.partial(total_kernel, n_ctx, n_dp), in_specs=[pl...  11.8 us
    pallas_call x1, Pallas kernels, head_grads(): pl.pallas_call(functools.partial(head_kernel, group, min(256, length)), g...  11.1 us
  transfers between devices with their start and end apart: 1, of which 0 were waited for; matrix products, arithmetic and copies ran while one was open for 0% of the time, Pallas kernels for 37%

commit v1 on v0

--- a/solution.py
+++ b/solution.py
@@ -135,16 +135,15 @@
     local.start()
 
     def piece(origin, rows, own):
-        start, size = rows
+        part = (pl.ds(*rows[:2]), pl.ds(*rows[2:]))
         if own:
-            return x_ref.at[pl.ds(start, size)]
-        return out_ref.at[origin, pl.ds(start, size)]
+            return x_ref.at[part]
+        return out_ref.at[(origin, *part)]
 
     def copy(line, way, origin, rows, own, send, recv):
-        start, size = rows
         return pltpu.make_async_remote_copy(
             src_ref=piece(origin, rows, own),
-            dst_ref=out_ref.at[origin, pl.ds(start, size)],
+            dst_ref=piece(origin, rows, False),
             send_sem=send,
             recv_sem=recv,
             device_id={"dp": neighbour(line, way)},
@@ -265,8 +264,6 @@
             send_b1(0, 0, c, way, always)
     for way in ways:
         send_b2(0, way)
-    for way in ways:
-        send_a2(0, 0, way)
     for step in range(slow - 1):
         for c in range(n_chunks):
             for way in ways:
@@ -275,15 +272,17 @@
                     send_a1(step + 1, c, way)
                 for way_b in ways:
                     send_b1(0, -way * (step + 1), c, way_b, present)
-        if step == 0:
-            for hop in range(fast - 1):
-                for way in ways:
-                    recv_b2(hop, way)
-                    if hop + 1 < fast - 1:
-                        send_b2(hop + 1, way)
-            for turn in range(1, fast):
-                for way in ways:
-                    send_a2(0, turn, way)
+    for way in ways:
+        send_a2(0, 0, way)
+    for hop in range(fast - 1):
+        for way in ways:
+            recv_b2(hop, way)
+            if hop + 1 < fast - 1:
+                send_b2(hop + 1, way)
+    for turn in range(1, fast):
+        for way in ways:
+            send_a2(0, turn, way)
+    for step in range(slow - 1):
         for turn in range(fast):
             for way in ways:
                 recv_a2(step, turn, way)
@@ -310,8 +309,14 @@
     slow = SLOW
     fast = devices // SLOW
     first = rows * 13 // 16 // 32 * 32
-    chunks = ((0, first // 2), (first // 2, first // 2))
-    tail = (first, rows - first)
+    half = first // 32 * 16
+    wide = columns // 2
+    chunks = tuple(
+        (start, size, column, wide)
+        for column in (0, wide)
+        for start, size in ((0, half), (half, first - half))
+    )
+    tail = (first, rows - first, 0, columns)
     n_chunks = len(chunks)
     dma = pltpu.SemaphoreType.DMA
     sizes = (
@@ -327,7 +332,7 @@
         out_shape=jax.ShapeDtypeStruct((devices, rows, columns), shard.dtype),
         scratch_shapes=[dma] + [dma((size,)) for size in sizes for _ in range(2)],
         compiler_params=pltpu.CompilerParams(
-            collective_id=collective_id, has_side_effects=True
+            collective_id=collective_id, has_side_effects=True, vmem_limit_bytes=2 * 1024 * 1024
         ),
         cost_estimate=pl.CostEstimate(
             flops=0, bytes_accessed=4 * devices * rows * columns, transcendentals=0

time: 371 us -> 362 us (0.976)
  Pallas kernels: 314 us -> 307 us
    pallas_call x2, Pallas kernels: 256 us -> 250 us  [gather_dp(): pl.pallas_call(functools.partial(gather_kernel, slow, fast, chunks, tail)...]
  transfers between devices with their start and end apart: 1 -> 1, of which waited for: 0 -> 0; matrix products, arithmetic and copies ran while one was open for 0% -> 0% of each run, Pallas kernels for 37% -> 38%
where the time goes in v1:
time: 362 us
  Pallas kernels  307 us (85%)
  matrix products  17.4 us (5%)
  local copies, waits for them, and re-layouts  15.9 us (4%)
  between operations  15.5 us (4%)
  other arithmetic  5.54 us (2%)
    pallas_call x2, Pallas kernels, gather_dp(): pl.pallas_call(functools.partial(gather_kernel, slow, fast, chunks, tail)...  250 us
    pallas_call x1, Pallas kernels, exchange(): pl.pallas_call(functools.partial(exchange_kernel, n_ctx, n_dp, widths, in...  34.8 us
    dot_general x1, matrix products, body(): lax.dot_general(input_rows, grouped_all, (((0, 1), (0, 1)), ((), ())), pr...  17.4 us
    unnamed x13, local copies, waits for them, and re-layouts  13.9 us
    pallas_call x1, Pallas kernels, total_over_devices(): pl.pallas_call(functools.partial(total_kernel, n_ctx, n_dp), in_specs=[pl...  11.6 us
    pallas_call x1, Pallas kernels, head_grads(): pl.pallas_call(functools.partial(head_kernel, group, min(256, length)), g...  11.1 us
  transfers between devices with their start and end apart: 1, of which 0 were waited for; matrix products, arithmetic and copies ran while one was open for 0% of the time, Pallas kernels for 38%

profile of v1, /device:TPU:0, one launch (start us, length us, event | category | flops | bytes accessed | tf_op | source)
XLA Modules:
  0.0 361.5 jit_solution(17862565793269577498)
XLA Ops:
  7.2 0.0 all-gather.2.cloned.1.call-start
  7.2 34.8 %exchange.1 = (bf16[512,1024]{1,0:T(8,128)(2,1)}, bf16[512,256]{1,0:T(8,128)(2,1)}, bf16[512,256]{1,0:T(8,128)(2,1)}, bf16[512,1024]{1,0:T(8,128)(2,1)}, bf16[8,128,512]{2,1,0:T(8,128)(2,1)}) custom-call(bf16[128,4096]{1,0:T(8,128)(2,1)} %bitcast.12, bf16[128,1024]{1,0:T(8,128)(2,1)} %bitcast.15, bf16[128,1024]{1,0:T(8,128)(2,1)} %bitcast.16, ...), custom_call_target="tpu_custom_call" | custom-call | bytes 4194304 | tf_op jit(solution)/shard_map/exchange/pallas_call | solution.py:445
  42.0 0.0 all-gather.2.cloned.1.call-update
  42.0 0.0 copy-start.1
  42.0 1.2 copy-done.1
  43.3 0.0 copy-start.2
  43.3 1.2 copy-done.2
  44.5 0.9 copy-done.3
  45.4 0.0 copy-start.4
  45.4 0.9 copy-done.4
  46.4 11.1 %head_grads.1.x_ref = bf16[512,1536]{1,0:T(8,128)(2,1)S(1)} custom-call(bf16[512,1024]{1,0:T(8,128)(2,1)S(1)} %copy-done.1, bf16[512,256]{1,0:T(8,128)(2,1)S(1)} %copy-done.3, bf16[512,256]{1,0:T(8,128)(2,1)S(1)} %copy-done.4, bf16[512,1024]{1,0:T(8,128)(2,1)S(1)} %copy-done.2), custom_call_target="tpu_custom_call" | custom-call | flops 2684354560 | bytes 4194304 | tf_op jit(solution)/shard_map/head_grads/pallas_call | solution.py:82
  57.5 0.0 copy-start.5
  57.5 124.8 %gather_grouped.1 = bf16[8,512,1536]{2,1,0:T(8,128)(2,1)S(1)} custom-call(bf16[512,1536]{1,0:T(8,128)(2,1)S(1)} %head_grads.1.x_ref), custom_call_target="tpu_custom_call" | custom-call | bytes 25165824 | tf_op jit(solution)/shard_map/gather_grouped/pallas_call | solution.py:328
  182.3 0.0 copy-start
  182.4 4.8 %copy-done = bf16[8,512,1536]{2,1,0:T(8,128)(2,1)} copy-done((bf16[8,512,1536]{2,1,0:T(8,128)(2,1)}, bf16[8,512,1536]{2,1,0:T(8,128)(2,1)S(1)}, u32[]{:S(2)}) %copy-start) | copy-done | bytes 12582936
  187.1 0.0 copy-done.5
  187.1 17.4 %multiply_reduce_fusion = (f32[]{:T(128)}, f32[512,1536]{1,0:T(8,128)}, f32[512,1536]{1,0:T(8,128)}, f32[512,1536]{1,0:T(8,128)}, f32[]{:T(128)}) fusion(f32[512,1536]{1,0:T(8,128)S(1)} %copy-done.5, f32[512,1536]{1,0:T(8,128)} %param.15, f32[512,1536]{1,0:T(8,128)} %param.14, bf16[8,512,512]{2,1,0:T(8,128)(2,1)} %all-gather.2.cloned.1.call-done, ...), kind=kOutput, calls=%fused_computation.4 | convolution fusion | flops 6455820288 | bytes 35651592 | tf_op jit(solution)/shard_map/dot_general | solution.py:556
  204.6 1.2 compare_select_fusion.1
  205.8 0.7 broadcast_in_dim.21.x_ref
  206.5 11.6 %total.1 = f32[8,128]{1,0:T(8,128)} custom-call(f32[8,128]{1,0:T(8,128)} %broadcast_in_dim.21.x_ref), custom_call_target="tpu_custom_call" | custom-call | bytes 65536 | tf_op jit(solution)/shard_map/total/pallas_call | solution.py:513
  218.1 1.3 fusion.2
  220.8 4.3 %subtract_convert_fusion = (bf16[512,1536]{1,0:T(8,128)(2,1)S(1)}, f32[512,1536]{1,0:T(8,128)}) fusion(f32[512,1536]{1,0:T(8,128)S(1)} %copy-done.5, f32[512,1536]{1,0:T(8,128)} %get-tuple-element.17, f32[]{:T(128)} %bitcast.6), kind=kLoop, calls=%fused_computation.3 | loop fusion | flops 3145728 | bytes 11010052 | tf_op jit(solution)/shard_map/convert_element_type | solution.py:576
  225.1 124.8 %gather_weights.1 = bf16[8,512,1536]{2,1,0:T(8,128)(2,1)S(1)} custom-call(bf16[512,1536]{1,0:T(8,128)(2,1)S(1)} %get-tuple-element.14.x_ref), custom_call_target="tpu_custom_call" | custom-call | bytes 25165824 | tf_op jit(solution)/shard_map/gather_weights/pallas_call | solution.py:328
  349.9 4.8 %copy.15 = bf16[4096,1536]{1,0:T(8,128)(2,1)} copy(bf16[4096,1536]{1,0:T(8,128)(2,1)S(1)} %bitcast.11) | data formatting | bytes 25165824
  (2 shorter events, 0.0 us)
Async XLA Ops:
  7.2 180.0 %all-gather.2.cloned.1.call-start = ((), (), s32[]{:S(2)}) async-start(), calls=%async_computation | async-start | bytes 5242880 | tf_op jit(solution)/shard_map/all_gather | solution.py:553
  42.0 1.2 copy-start.1
  43.3 1.2 copy-start.2
  44.5 0.9 copy-start.3
  45.4 0.9 copy-start.4
  57.5 129.6 %copy-start.5 = (f32[512,1536]{1,0:T(8,128)S(1)}, f32[512,1536]{1,0:T(8,128)}, u32[]{:S(2)}) copy-start(f32[512,1536]{1,0:T(8,128)} %param.13) | copy-start | bytes 9437188
  182.3 4.8 %copy-start = (bf16[8,512,1536]{2,1,0:T(8,128)(2,1)}, bf16[8,512,1536]{2,1,0:T(8,128)(2,1)S(1)}, u32[]{:S(2)}) copy-start(bf16[8,512,1536]{2,1,0:T(8,128)(2,1)S(1)} %gather_grouped.1) | copy-start | bytes 37748740
Sparse Core Ops, SparseCore 0:
  42.2 33.7 all-gather.1

commit v2 on v1

--- a/solution.py
+++ b/solution.py
@@ -32,73 +32,49 @@
     return jnp.dot(left, right, preferred_element_type=jnp.float32)
 
 
-def head_kernel(group, block, q_ref, k_ref, v_ref, g_ref, out_ref, dk_acc, dv_acc):
-    head = pl.program_id(1)
+def head_grads(group, block, kv, q_ref, k_ref, v_ref, g_ref, out_ref, dk_acc, dv_acc):
     length = q_ref.shape[0]
     scale = HEAD_DIM ** (-0.5)
-
-    @pl.when(head == 0)
-    def _():
-        dk_acc[...] = jnp.zeros_like(dk_acc)
-        dv_acc[...] = jnp.zeros_like(dv_acc)
-
-    for start in range(0, length, block):
-        keys = start + block
-        query = q_ref[start:keys, :]
-        grad = g_ref[start:keys, :]
-        key = k_ref[:keys, :]
-        value = v_ref[:keys, :]
-        scores = nt(key, query) * scale
-        row = lax.broadcasted_iota(jnp.int32, (keys, block), 0)
-        column = lax.broadcasted_iota(jnp.int32, (keys, block), 1) + start
-        scores = jnp.where(row <= column, scores, masked_score)
-        weights = jnp.exp(scores - jnp.max(scores, axis=0, keepdims=True))
-        probs = weights / jnp.sum(weights, axis=0, keepdims=True)
-        probs_b = probs.astype(jnp.bfloat16)
-        prob_grad = nt(value, grad)
-        row_delta = jnp.sum(probs_b.astype(jnp.float32) * prob_grad, axis=0, keepdims=True)
-        dscore = (probs * (prob_grad - row_delta)).astype(jnp.bfloat16)
-        dq = lax.dot_general(
-            dscore, key, (((0,), (0,)), ((), ())), preferred_element_type=jnp.float32
-        )
-        column_start = pl.multiple_of(head * HEAD_DIM, HEAD_DIM)
-        out_ref[start:keys, pl.ds(column_start, HEAD_DIM)] = (dq * scale).astype(jnp.bfloat16)
-        dk_acc[:keys, :] += nn(dscore, query)
-        dv_acc[:keys, :] += nn(probs_b, grad)
-
-    @pl.when(head == group - 1)
-    def _():
-        width = group * HEAD_DIM
-        out_ref[:, width : width + HEAD_DIM] = (dk_acc[...] * scale).astype(jnp.bfloat16)
-        out_ref[:, width + HEAD_DIM :] = dv_acc[...].astype(jnp.bfloat16)
-
-
-def head_grads(query, key, value, grad):
-    length = query.shape[0]
-    kv_local = key.shape[1] // HEAD_DIM
-    group = query.shape[1] // key.shape[1]
-    query_spec = pl.BlockSpec((length, HEAD_DIM), lambda g, h: (0, g * group + h))
-    key_spec = pl.BlockSpec((length, HEAD_DIM), lambda g, h: (0, g))
-    return pl.pallas_call(
-        functools.partial(head_kernel, group, min(256, length)),
-        grid=(kv_local, group),
-        in_specs=[query_spec, key_spec, key_spec, query_spec],
-        out_specs=pl.BlockSpec((length, (group + 2) * HEAD_DIM), lambda g, h: (0, g)),
-        out_shape=jax.ShapeDtypeStruct(
-            (length, kv_local * (group + 2) * HEAD_DIM), jnp.bfloat16
-        ),
-        scratch_shapes=[pltpu.VMEM((length, HEAD_DIM), jnp.float32)] * 2,
-        compiler_params=pltpu.CompilerParams(vmem_limit_bytes=40 * 1024 * 1024),
-        cost_estimate=pl.CostEstimate(
-            flops=10 * length * length * query.shape[1],
-            bytes_accessed=8 * length * query.shape[1],
-            transcendentals=length * length * kv_local * group,
-        ),
-        name="head_grads",
-    )(query, key, value, grad)
-
-
-def gather_kernel(slow, fast, chunks, tail, x_ref, out_ref, *sems):
+    width = group * HEAD_DIM
+    base = kv * (width + 2 * HEAD_DIM)
+    kv_columns = slice(kv * HEAD_DIM, (kv + 1) * HEAD_DIM)
+    dk_acc[...] = jnp.zeros_like(dk_acc)
+    dv_acc[...] = jnp.zeros_like(dv_acc)
+
+    def one_head(head, carry):
+        here = pl.ds(pl.multiple_of(kv * width + head * HEAD_DIM, HEAD_DIM), HEAD_DIM)
+        there = pl.ds(pl.multiple_of(base + head * HEAD_DIM, HEAD_DIM), HEAD_DIM)
+        for start in range(0, length, block):
+            keys = start + block
+            query = q_ref[start:keys, here]
+            grad = g_ref[start:keys, here]
+            key = k_ref[:keys, kv_columns]
+            value = v_ref[:keys, kv_columns]
+            scores = nt(key, query) * scale
+            row = lax.broadcasted_iota(jnp.int32, (keys, block), 0)
+            column = lax.broadcasted_iota(jnp.int32, (keys, block), 1) + start
+            scores = jnp.where(row <= column, scores, masked_score)
+            weights = jnp.exp(scores - jnp.max(scores, axis=0, keepdims=True))
+            probs = weights / jnp.sum(weights, axis=0, keepdims=True)
+            probs_b = probs.astype(jnp.bfloat16)
+            prob_grad = nt(value, grad)
+            row_delta = jnp.sum(probs_b.astype(jnp.float32) * prob_grad, axis=0, keepdims=True)
+            dscore = (probs * (prob_grad - row_delta)).astype(jnp.bfloat16)
+            dq = lax.dot_general(
+                dscore, key, (((0,), (0,)), ((), ())), preferred_element_type=jnp.float32
+            )
+            out_ref[start:keys, there] = (dq * scale).astype(jnp.bfloat16)
+            dk_acc[:keys, :] += nn(dscore, query)
+            dv_acc[:keys, :] += nn(probs_b, grad)
+        return carry
+
+    lax.fori_loop(0, group, one_head, 0)
+    split = base + width
+    out_ref[:, split : split + HEAD_DIM] = (dk_acc[...] * scale).astype(jnp.bfloat16)
+    out_ref[:, split + HEAD_DIM : split + 2 * HEAD_DIM] = dv_acc[...].astype(jnp.bfloat16)
+
+
+def gather_kernel(slow, fast, chunks, tail, x_ref, out_ref, *sems, enter=None, produce=None, relay=None):
     local_sem, p1s, p1r, x1s, x1r, x2s, x2r, p2s, p2r = sems
     me = lax.axis_index("dp")
     a = me // fast
@@ -113,26 +89,28 @@
         pos, size, _ = lines[line]
         return pos + 1 < size if way > 0 else pos > 0
 
-    barrier = pltpu.get_barrier_semaphore()
-    for line in ("a", "b"):
-        for way in (1, -1):
-
-            @pl.when(can(line, way))
-            def _(line=line, way=way):
-                pl.semaphore_signal(
-                    barrier,
-                    inc=1,
-                    device_id={"dp": neighbour(line, way)},
-                    device_id_type=MESH_ID,
-                )
-
-    neighbours = sum(
-        can(line, way).astype(jnp.int32) for line in ("a", "b") for way in (1, -1)
-    )
-    pl.semaphore_wait(barrier, neighbours)
+    if enter is None:
+        barrier = pltpu.get_barrier_semaphore()
+        for line in ("a", "b"):
+            for way in (1, -1):
+
+                @pl.when(can(line, way))
+                def _(line=line, way=way):
+                    pl.semaphore_signal(
+                        barrier,
+                        inc=1,
+                        device_id={"dp": neighbour(line, way)},
+                        device_id_type=MESH_ID,
+                    )
+
+        neighbours = sum(
+            can(line, way).astype(jnp.int32) for line in ("a", "b") for way in (1, -1)
+        )
+        pl.semaphore_wait(barrier, neighbours)
+    else:
+        enter()
 
     local = pltpu.make_async_copy(x_ref, out_ref.at[me], local_sem)
-    local.start()
 
     def piece(origin, rows, own):
         part = (pl.ds(*rows[:2]), pl.ds(*rows[2:]))
@@ -258,12 +236,17 @@
     ways = (1, -1)
     always = a >= 0
     for c in range(n_chunks):
+        if produce is not None:
+            produce(chunks[c][2] + chunks[c][3])
         for way in ways:
             send_a1(0, c, way)
         for way in ways:
             send_b1(0, 0, c, way, always)
+    local.start()
     for way in ways:
         send_b2(0, way)
+    if relay is not None:
+        relay()
     for step in range(slow - 1):
         for c in range(n_chunks):
             for way in ways:
@@ -304,8 +287,7 @@
             copy(*args).wait_send()
 
 
-def gather_dp(shard, devices, collective_id, name):
-    rows, columns = shard.shape
+def gather_plan(rows, columns, devices):
     slow = SLOW
     fast = devices // SLOW
     first = rows * 13 // 16 // 32 * 32
@@ -325,12 +307,19 @@
         2 * (fast - 1),
         2 * (slow - 1) * fast,
     )
+    semaphores = [dma] + [dma((size,)) for size in sizes for _ in range(2)]
+    return (slow, fast, chunks, tail), semaphores
+
+
+def gather_dp(shard, devices, collective_id, name):
+    rows, columns = shard.shape
+    shape, semaphores = gather_plan(rows, columns, devices)
     return pl.pallas_call(
-        functools.partial(gather_kernel, slow, fast, chunks, tail),
+        functools.partial(gather_kernel, *shape),
         in_specs=[pl.BlockSpec(memory_space=pl.ANY)],
         out_specs=pl.BlockSpec(memory_space=pl.ANY),
         out_shape=jax.ShapeDtypeStruct((devices, rows, columns), shard.dtype),
-        scratch_shapes=[dma] + [dma((size,)) for size in sizes for _ in range(2)],
+        scratch_shapes=semaphores,
         compiler_params=pltpu.CompilerParams(
             collective_id=collective_id, has_side_effects=True, vmem_limit_bytes=2 * 1024 * 1024
         ),
@@ -341,127 +330,179 @@
     )(shard)
 
 
-def exchange_kernel(n_ctx, n_dp, widths, input_width, *refs):
+def front_kernel(n_ctx, n_dp, widths, input_width, shape, *refs):
     count = len(widths)
     sources, source_input = refs[:count], refs[count]
-    targets, target_input = refs[count + 1 : 2 * count + 1], refs[2 * count + 1]
-    ctx_send, ctx_recv, dp_send, dp_recv, local_sems = refs[2 * count + 2 :]
+    out_ref, target_input = refs[count + 1 : count + 3]
+    targets = refs[count + 3 : 2 * count + 3]
+    rest = refs[2 * count + 3 :]
+    grouped, dk_acc, dv_acc, ctx_send, ctx_recv, dp_send, dp_recv, token_send, token_recv = rest[:9]
+    local_sems = rest[9]
     dp = lax.axis_index("dp")
     ctx = lax.axis_index("ctx")
     rows = source_input.shape[0]
-    barrier = pltpu.get_barrier_semaphore()
-    for turn in range(1, n_ctx):
-        pl.semaphore_signal(
-            barrier, inc=1, device_id={"ctx": lax.rem(ctx + turn, n_ctx)}, device_id_type=MESH_ID
-        )
-    for turn in range(1, n_dp):
-        pl.semaphore_signal(
-            barrier, inc=1, device_id={"dp": lax.rem(dp + turn, n_dp)}, device_id_type=MESH_ID
-        )
-    pl.semaphore_wait(barrier, n_ctx + n_dp - 2)
-
-    def source(i, peer):
-        return sources[i].at[:, pl.ds(pl.multiple_of(peer * widths[i], 128), widths[i])]
+    kv_local = widths[1] // HEAD_DIM
+    group = widths[0] // widths[1]
+    steps = tuple(width // kv_local for width in widths)
+    remote = []
+
+    def source(i, kv, peer):
+        start = pl.multiple_of(peer * widths[i] + kv * steps[i], 128)
+        return sources[i].at[:, pl.ds(start, steps[i])]
+
+    def target(i, kv, owner):
+        start = pl.multiple_of(owner * rows, 16)
+        return targets[i].at[pl.ds(start, rows), pl.ds(kv * steps[i], steps[i])]
 
     def source_columns(peer):
         return source_input.at[:, pl.ds(pl.multiple_of(peer * input_width, 128), input_width)]
 
-    def row_block(i, owner):
-        return targets[i].at[pl.ds(pl.multiple_of(owner * rows, 16), rows)]
-
-    copies = []
-    for turn in range(1, n_ctx):
-        peer = lax.rem(ctx + turn, n_ctx)
-        for i in range(count):
-            k = i * (n_ctx - 1) + turn - 1
-            copies.append(
-                pltpu.make_async_remote_copy(
-                    src_ref=source(i, peer),
-                    dst_ref=row_block(i, ctx),
-                    send_sem=ctx_send.at[k],
-                    recv_sem=ctx_recv.at[k],
-                    device_id={"ctx": peer},
+    def input_block(owner):
+        return target_input.at[owner, pl.ds(pl.multiple_of(ctx * rows, 16), rows)]
+
+    def input_tokens(owner):
+        return target_input.at[:, pl.ds(pl.multiple_of(owner * rows, 16), rows)]
+
+    def token_copy(turn, peer, owner):
+        return pltpu.make_async_remote_copy(
+            src_ref=input_tokens(owner),
+            dst_ref=input_tokens(owner),
+            send_sem=token_send.at[turn - 1],
+            recv_sem=token_recv.at[turn - 1],
+            device_id={"ctx": peer},
+            device_id_type=MESH_ID,
+        )
+
+    def ctx_copy(i, kv, turn, peer, owner):
+        k = (kv * count + i) * (n_ctx - 1) + turn - 1
+        return pltpu.make_async_remote_copy(
+            src_ref=source(i, kv, peer),
+            dst_ref=target(i, kv, owner),
+            send_sem=ctx_send.at[k],
+            recv_sem=ctx_recv.at[k],
+            device_id={"ctx": peer},
+            device_id_type=MESH_ID,
+        )
+
+    def input_copy(turn, peer, owner):
+        return pltpu.make_async_remote_copy(
+            src_ref=source_columns(peer),
+            dst_ref=input_block(owner),
+            send_sem=dp_send.at[turn - 1],
+            recv_sem=dp_recv.at[turn - 1],
+            device_id={"dp": peer},
+            device_id_type=MESH_ID,
+        )
+
+    def own(i, kv):
+        return pltpu.make_async_copy(
+            source(i, kv, ctx), target(i, kv, ctx), local_sems.at[kv * count + i]
+        )
+
+    own_input = pltpu.make_async_copy(
+        source_columns(dp), input_block(dp), local_sems.at[kv_local * count]
+    )
+
+    def enter():
+        barrier = pltpu.get_barrier_semaphore()
+        for axis, me, size in (("ctx", ctx, n_ctx), ("dp", dp, n_dp)):
+            for turn in range(1, size):
+                pl.semaphore_signal(
+                    barrier,
+                    inc=1,
+                    device_id={axis: lax.rem(me + turn, size)},
                     device_id_type=MESH_ID,
                 )
-            )
-            copies[-1].start()
-    for turn in range(1, n_dp):
-        peer = lax.rem(dp + turn, n_dp)
-        copies.append(
-            pltpu.make_async_remote_copy(
-                src_ref=source_columns(peer),
-                dst_ref=target_input.at[dp],
-                send_sem=dp_send.at[turn - 1],
-                recv_sem=dp_recv.at[turn - 1],
-                device_id={"dp": peer},
-                device_id_type=MESH_ID,
-            )
-        )
-        copies[-1].start()
-    owns = [
-        pltpu.make_async_copy(source(i, ctx), row_block(i, ctx), local_sems.at[i])
-        for i in range(count)
-    ]
-    owns.append(
-        pltpu.make_async_copy(source_columns(dp), target_input.at[dp], local_sems.at[count])
-    )
-    for own in owns:
-        own.start()
-    for own in owns:
-        own.wait()
+        pl.semaphore_wait(barrier, n_ctx + n_dp - 2)
+        for kv in range(kv_local):
+            for i in range(count):
+                for turn in range(1, n_ctx):
+                    copy = ctx_copy(i, kv, turn, lax.rem(ctx + turn, n_ctx), ctx)
+                    copy.start()
+                    remote.append(copy)
+                own(i, kv).start()
+        for turn in range(1, n_dp):
+            copy = input_copy(turn, lax.rem(dp + turn, n_dp), dp)
+            copy.start()
+            remote.append(copy)
+        own_input.start()
+
+    made = []
+
+    def produce(column):
+        while len(made) * (group + 2) * HEAD_DIM < column:
+            kv = len(made)
+            for i in range(count):
+                own(i, kv).wait()
+                for turn in range(1, n_ctx):
+                    origin = lax.rem(ctx + n_ctx - turn, n_ctx)
+                    ctx_copy(i, kv, turn, origin, origin).wait_recv()
+            block = min(256, rows * n_ctx)
+            head_grads(group, block, kv, *targets, grouped, dk_acc, dv_acc)
+            made.append(kv)
+
+    def relay():
+        own_input.wait()
+        for turn in range(1, n_dp):
+            origin = lax.rem(dp + n_dp - turn, n_dp)
+            input_copy(turn, origin, origin).wait_recv()
+        for turn in range(1, n_ctx):
+            copy = token_copy(turn, lax.rem(ctx + turn, n_ctx), ctx)
+            copy.start()
+            remote.append(copy)
+
+    gather_kernel(
+        *shape, grouped, out_ref, *rest[10:], enter=enter, produce=produce, relay=relay
+    )
     for turn in range(1, n_ctx):
         origin = lax.rem(ctx + n_ctx - turn, n_ctx)
-        for i in range(count):
-            k = i * (n_ctx - 1) + turn - 1
-            pltpu.make_async_remote_copy(
-                src_ref=source(i, origin),
-                dst_ref=row_block(i, origin),
-                send_sem=ctx_send.at[k],
-                recv_sem=ctx_recv.at[k],
-                device_id={"ctx": origin},
-                device_id_type=MESH_ID,
-            ).wait_recv()
-    for turn in range(1, n_dp):
-        origin = lax.rem(dp + n_dp - turn, n_dp)
-        pltpu.make_async_remote_copy(
-            src_ref=source_columns(origin),
-            dst_ref=target_input.at[origin],
-            send_sem=dp_send.at[turn - 1],
-            recv_sem=dp_recv.at[turn - 1],
-            device_id={"dp": origin},
-            device_id_type=MESH_ID,
-        ).wait_recv()
-    for copy in copies:
+        token_copy(turn, origin, origin).wait_recv()
+    for copy in remote:
         copy.wait_send()
 
 
-def exchange(arrays, layer_input, n_ctx, n_dp):
+def front(arrays, layer_input, n_ctx, n_dp):
     rows = layer_input.shape[0]
+    length = rows * n_ctx
     widths = tuple(array.shape[1] // n_ctx for array in arrays)
     input_width = layer_input.shape[1] // n_dp
+    columns = widths[0] + 2 * widths[1]
+    kv_local = widths[1] // HEAD_DIM
+    shape, semaphores = gather_plan(length, columns, n_dp)
     dma = pltpu.SemaphoreType.DMA
-    ctx_copies = len(arrays) * (n_ctx - 1)
+    ctx_copies = len(arrays) * (n_ctx - 1) * kv_local
     anywhere = pl.BlockSpec(memory_space=pl.ANY)
     return pl.pallas_call(
-        functools.partial(exchange_kernel, n_ctx, n_dp, widths, input_width),
+        functools.partial(front_kernel, n_ctx, n_dp, widths, input_width, shape),
         in_specs=[anywhere] * (len(arrays) + 1),
-        out_specs=[anywhere] * (len(arrays) + 1),
+        out_specs=[anywhere] * 2,
         out_shape=[
-            jax.ShapeDtypeStruct((rows * n_ctx, width), jnp.bfloat16) for width in widths
-        ]
-        + [jax.ShapeDtypeStruct((n_dp, rows, input_width), jnp.bfloat16)],
-        scratch_shapes=[
+            jax.ShapeDtypeStruct((n_dp, length, columns), jnp.bfloat16),
+            jax.ShapeDtypeStruct((n_dp, length, input_width), jnp.bfloat16),
+        ],
+        scratch_shapes=[pltpu.VMEM((length, width), jnp.bfloat16) for width in widths]
+        + [
+            pltpu.VMEM((length, columns), jnp.bfloat16),
+            pltpu.VMEM((length, HEAD_DIM), jnp.float32),
+            pltpu.VMEM((length, HEAD_DIM), jnp.float32),
             dma((ctx_copies,)),
             dma((ctx_copies,)),
             dma((n_dp - 1,)),
             dma((n_dp - 1,)),
-            dma((len(arrays) + 1,)),
-        ],
-        compiler_params=pltpu.CompilerParams(collective_id=3, has_side_effects=True),
+            dma((n_ctx - 1,)),
+            dma((n_ctx - 1,)),
+            dma((len(arrays) * kv_local + 1,)),
+        ]
+        + semaphores,
+        compiler_params=pltpu.CompilerParams(
+            collective_id=3, has_side_effects=True, vmem_limit_bytes=28 * 1024 * 1024
+        ),
         cost_estimate=pl.CostEstimate(
-            flops=0, bytes_accessed=8 * rows * layer_input.shape[1], transcendentals=0
+            flops=10 * length * length * widths[0],
+            bytes_accessed=4 * n_dp * length * columns,
+            transcendentals=length * length * widths[0] // HEAD_DIM,
         ),
-        name="exchange",
+        name="front",
     )(*arrays, layer_input)
 
 
@@ -544,15 +585,12 @@
     second_moment,
 ):
     weight_sq = jnp.sum(master_weight * master_weight)
-    *heads, input_rows = exchange(
+    grouped_all, input_rows = front(
         (queries[0], keys_saved[0], values_saved[0], out_grad[0]),
         layer_input[0],
         heads_split,
         devices,
     )
-    input_rows = lax.all_gather(input_rows, "ctx", axis=1, tiled=True)
-    grouped = head_grads(*heads)
-    grouped_all = gather_dp(grouped, devices, 1, "gather_grouped")
     gradient = lax.dot_general(
         input_rows,
         grouped_all,

time: 362 us -> 324 us (0.90)
  Pallas kernels: 307 us -> 288 us
  between operations: 15.5 us -> 2.03 us
    pallas_call x4 -> x2, Pallas kernels: 296 us -> 275 us  [the longest x1 149 us: front(): pl.pallas_call(functools.partial(front_kernel, n_ctx, n_dp, widths, input...]
    unnamed x13 -> x11, local copies, waits for them, and re-layouts: 13.9 us -> 10.3 us
  transfers between devices with their start and end apart: 1 -> 0, of which waited for: 0 -> 0; matrix products, arithmetic and copies ran while one was open for 0% -> 0% of each run, Pallas kernels for 38% -> 0%
where the time goes in v2:
time: 324 us; the launch traced here: 323 us
  Pallas kernels  288 us (89%)
  matrix products  14.5 us (4%)
  local copies, waits for them, and re-layouts  12.3 us (4%)
  other arithmetic  6.53 us (2%)
    pallas_call x1, Pallas kernels, front(): pl.pallas_call(functools.partial(front_kernel, n_ctx, n_dp, widths, input...  149 us
    pallas_call x1, Pallas kernels, gather_dp(): pl.pallas_call(functools.partial(gather_kernel, *shape), in_specs=[pl.Blo...  125 us
    dot_general x1, matrix products, body(): lax.dot_general(input_rows, grouped_all, (((0, 1), (0, 1)), ((), ())), pr...  14.5 us
    pallas_call x1, Pallas kernels, total_over_devices(): pl.pallas_call(functools.partial(total_kernel, n_ctx, n_dp), in_specs=[pl...  13.1 us
    unnamed x11, local copies, waits for them, and re-layouts  10.3 us

profile of v2, /device:TPU:0, one launch (start us, length us, event | category | flops | bytes accessed | tf_op | source)
XLA Modules:
  0.0 323.3 jit_solution(12412317214067732277)
XLA Ops:
  0.6 0.0 copy-start
  0.6 1.2 copy-done
  1.9 0.0 copy-start.1
  1.9 1.2 copy-done.1
  3.1 0.0 copy-start.2
  3.1 1.2 copy-done.2
  4.3 0.0 copy-start.3
  4.3 0.9 copy-done.3
  5.3 0.0 copy-start.4
  5.3 0.9 copy-done.4
  6.2 149.4 %front.1 = (bf16[8,512,1536]{2,1,0:T(8,128)(2,1)S(1)}, bf16[8,512,512]{2,1,0:T(8,128)(2,1)S(1)}) custom-call(bf16[128,4096]{1,0:T(8,128)(2,1)S(1)} %bitcast.12, bf16[128,1024]{1,0:T(8,128)(2,1)S(1)} %bitcast.15, bf16[128,1024]{1,0:T(8,128)(2,1)S(1)} %bitcast.16, bf16[128,4096]{1,0:T(8,128)(2,1)S(1)} %bitcast.13, bf16[128,4096]{1,0:T(8,128)(2,1)S(1)} %bitcast.14), custom_call_target="tpu_custom_call" | custom-call | flops 2684354560 | bytes 25165824 | tf_op jit(solution)/shard_map/front/pallas_call | solution.py:475
  155.6 14.5 %multiply_reduce_fusion = (f32[]{:T(128)}, f32[512,1536]{1,0:T(8,128)}, f32[512,1536]{1,0:T(8,128)}, f32[512,1536]{1,0:T(8,128)}, f32[]{:T(128)}) fusion(f32[512,1536]{1,0:T(8,128)} %param.13, f32[512,1536]{1,0:T(8,128)} %param.15, f32[512,1536]{1,0:T(8,128)} %param.14, bf16[8,512,512]{2,1,0:T(8,128)(2,1)S(1)} %get-tuple-element.6, ...), kind=kOutput, calls=%fused_computation.4 | convolution fusion | flops 6455820288 | bytes 35651592 | tf_op jit(solution)/shard_map/dot_general | solution.py:594
  170.2 1.3 compare_select_fusion.1
  171.4 0.7 broadcast_in_dim.21.x_ref
  172.1 13.1 %total.1 = f32[8,128]{1,0:T(8,128)} custom-call(f32[8,128]{1,0:T(8,128)} %broadcast_in_dim.21.x_ref), custom_call_target="tpu_custom_call" | custom-call | bytes 65536 | tf_op jit(solution)/shard_map/total/pallas_call | solution.py:554
  185.2 1.3 fusion.2
  187.8 5.3 %subtract_convert_fusion = (bf16[512,1536]{1,0:T(8,128)(2,1)S(1)}, f32[512,1536]{1,0:T(8,128)}) fusion(f32[512,1536]{1,0:T(8,128)} %param.13, f32[512,1536]{1,0:T(8,128)} %get-tuple-element.11, f32[]{:T(128)} %bitcast.6), kind=kLoop, calls=%fused_computation.3 | loop fusion | flops 3145728 | bytes 11010052 | tf_op jit(solution)/shard_map/convert_element_type | solution.py:614
  193.1 125.5 %gather_weights.1 = bf16[8,512,1536]{2,1,0:T(8,128)(2,1)S(1)} custom-call(bf16[512,1536]{1,0:T(8,128)(2,1)S(1)} %get-tuple-element.8.x_ref), custom_call_target="tpu_custom_call" | custom-call | bytes 25165824 | tf_op jit(solution)/shard_map/gather_weights/pallas_call | solution.py:317
  318.6 4.8 %copy.15 = bf16[4096,1536]{1,0:T(8,128)(2,1)} copy(bf16[4096,1536]{1,0:T(8,128)(2,1)S(1)} %bitcast.11) | data formatting | bytes 25165824
Async XLA Ops:
  0.6 1.2 copy-start
  1.9 1.2 copy-start.1
  3.1 1.2 copy-start.2
  4.3 0.9 copy-start.3
  5.3 0.9 copy-start.4

commit v3 on v2

--- a/solution.py
+++ b/solution.py
@@ -495,7 +495,7 @@
         ]
         + semaphores,
         compiler_params=pltpu.CompilerParams(
-            collective_id=3, has_side_effects=True, vmem_limit_bytes=28 * 1024 * 1024
+            collective_id=3, has_side_effects=True, vmem_limit_bytes=50 * 1024 * 1024
         ),
         cost_estimate=pl.CostEstimate(
             flops=10 * length * length * widths[0],

time: 324 us -> 324 us (level)
    unnamed x11 -> x17, local copies, waits for them, and re-layouts: 10.3 us -> 10.4 us
where the time goes in v3:
time: 324 us
  Pallas kernels  288 us (89%)
  matrix products  16.1 us (5%)
  local copies, waits for them, and re-layouts  12.3 us (4%)
  other arithmetic  5.53 us (2%)
    pallas_call x1, Pallas kernels, front(): pl.pallas_call(functools.partial(front_kernel, n_ctx, n_dp, widths, input...  149 us
    pallas_call x1, Pallas kernels, gather_dp(): pl.pallas_call(functools.partial(gather_kernel, *shape), in_specs=[pl.Blo...  125 us
    dot_general x1, matrix products, body(): lax.dot_general(input_rows, grouped_all, (((0, 1), (0, 1)), ((), ())), pr...  16.1 us
    pallas_call x1, Pallas kernels, total_over_devices(): pl.pallas_call(functools.partial(total_kernel, n_ctx, n_dp), in_specs=[pl...  13.2 us
    unnamed x17, local copies, waits for them, and re-layouts  10.4 us

profile of v3, /device:TPU:0, one launch (start us, length us, event | category | flops | bytes accessed | tf_op | source)
XLA Modules:
  0.0 324.0 jit_solution(15021179066249284725)
XLA Ops:
  0.6 0.0 copy-start
  0.6 1.2 copy-done
  1.9 0.0 copy-start.1
  1.9 1.2 copy-done.1
  3.1 0.0 copy-start.2
  3.1 1.2 copy-done.2
  4.3 0.0 copy-start.3
  4.3 0.9 copy-done.3
  5.3 0.9 copy-done.4
  6.2 0.0 copy-start.5
  6.2 0.0 copy-start.6
  6.2 0.0 copy-start.7
  6.2 149.5 %front.1 = (bf16[8,512,1536]{2,1,0:T(8,128)(2,1)}, bf16[8,512,512]{2,1,0:T(8,128)(2,1)}) custom-call(bf16[128,4096]{1,0:T(8,128)(2,1)S(1)} %bitcast.12, bf16[128,1024]{1,0:T(8,128)(2,1)S(1)} %bitcast.15, bf16[128,1024]{1,0:T(8,128)(2,1)S(1)} %bitcast.16, bf16[128,4096]{1,0:T(8,128)(2,1)S(1)} %bitcast.13, bf16[128,4096]{1,0:T(8,128)(2,1)S(1)} %bitcast.14), custom_call_target="tpu_custom_call" | custom-call | flops 2684354560 | bytes 25165824 | tf_op jit(solution)/shard_map/front/pallas_call | solution.py:475
  155.7 0.0 copy-done.5
  155.7 0.0 copy-done.6
  155.7 0.0 copy-done.7
  155.7 16.1 %multiply_reduce_fusion = (f32[]{:T(128)}, f32[512,1536]{1,0:T(8,128)}, f32[512,1536]{1,0:T(8,128)}, f32[512,1536]{1,0:T(8,128)}, f32[]{:T(128)}) fusion(f32[512,1536]{1,0:T(8,128)S(1)} %copy-done.5, f32[512,1536]{1,0:T(8,128)S(1)} %copy-done.6, f32[512,1536]{1,0:T(8,128)S(1)} %copy-done.7, bf16[8,512,512]{2,1,0:T(8,128)(2,1)} %get-tuple-element.6, ...), kind=kOutput, calls=%fused_computation.4 | convolution fusion | flops 6455820288 | bytes 35651592 | tf_op jit(solution)/shard_map/dot_general | solution.py:594
  171.8 1.2 compare_select_fusion.1
  173.0 0.7 broadcast_in_dim.21.x_ref
  173.6 13.2 %total.1 = f32[8,128]{1,0:T(8,128)} custom-call(f32[8,128]{1,0:T(8,128)} %broadcast_in_dim.21.x_ref), custom_call_target="tpu_custom_call" | custom-call | bytes 65536 | tf_op jit(solution)/shard_map/total/pallas_call | solution.py:554
  186.8 1.3 fusion.2
  189.4 4.3 %subtract_convert_fusion = (bf16[512,1536]{1,0:T(8,128)(2,1)S(1)}, f32[512,1536]{1,0:T(8,128)}) fusion(f32[512,1536]{1,0:T(8,128)S(1)} %copy-done.5, f32[512,1536]{1,0:T(8,128)} %get-tuple-element.11, f32[]{:T(128)} %bitcast.6), kind=kLoop, calls=%fused_computation.3 | loop fusion | flops 3145728 | bytes 11010052 | tf_op jit(solution)/shard_map/convert_element_type | solution.py:614
  193.7 125.5 %gather_weights.1 = bf16[8,512,1536]{2,1,0:T(8,128)(2,1)S(1)} custom-call(bf16[512,1536]{1,0:T(8,128)(2,1)S(1)} %get-tuple-element.8.x_ref), custom_call_target="tpu_custom_call" | custom-call | bytes 25165824 | tf_op jit(solution)/shard_map/gather_weights/pallas_call | solution.py:317
  319.2 4.8 %copy.15 = bf16[4096,1536]{1,0:T(8,128)(2,1)} copy(bf16[4096,1536]{1,0:T(8,128)(2,1)S(1)} %bitcast.11) | data formatting | bytes 25165824
  (1 shorter events, 0.0 us)
Async XLA Ops:
  0.6 1.2 copy-start
  1.9 1.2 copy-start.1
  3.1 1.2 copy-start.2
  4.3 0.9 copy-start.3
  5.3 0.9 copy-start.4
  6.2 149.5 %copy-start.5 = (f32[512,1536]{1,0:T(8,128)S(1)}, f32[512,1536]{1,0:T(8,128)}, u32[]{:S(2)}) copy-start(f32[512,1536]{1,0:T(8,128)} %param.13) | copy-start | bytes 9437188
  6.2 149.5 %copy-start.6 = (f32[512,1536]{1,0:T(8,128)S(1)}, f32[512,1536]{1,0:T(8,128)}, u32[]{:S(2)}) copy-start(f32[512,1536]{1,0:T(8,128)} %param.15) | copy-start | bytes 9437188
  6.2 149.5 %copy-start.7 = (f32[512,1536]{1,0:T(8,128)S(1)}, f32[512,1536]{1,0:T(8,128)}, u32[]{:S(2)}) copy-start(f32[512,1536]{1,0:T(8,128)} %param.14) | copy-start | bytes 9437188
